TPU v7x, 256 devices: a whole 4x4x8 slice. The times are simulated.
256 devices in a mesh: mem: 8 (over x_hi, y), grid: 32 (over z, x_lo, core).
Axes of the slice: x: 4 (x_hi: 2, x_lo: 2; x = x_hi * 2 + x_lo), y: 4, z: 8, core: 2. Of those that a mesh axis runs over, the one named last changes fastest.
Arguments:
- ensemble: bfloat16 [1024, 1024, 1024], P(('mem', 'grid')), may hold values from -6 to 6
- right_side: float32 [1024, 1024], P(('mem', 'grid')), may hold values from -18 to 18
- obs_prec: float32 [1024, 1024], P(('mem', 'grid')), may hold values from 0.5 to 2
- neighbors: int32 [1024, 8], replicated, may hold values from 0 to 1023, as said below
- loc_weight: float32 [1024, 8], replicated, may hold values from 0 to 0.08
Outputs:
- solution_field: float32 [1024, 1024], P(('mem', 'grid'))
- residual: float32 [1024, 1024], P(('mem', 'grid'))
Inputs may be any that keep to these rules, and one draw needn't show every extreme that they name: neighbors[b, j] lies within 3 of b along the cyclic order of blocks, and every block is listed exactly once in each of the 8 columns.
All inputs are finite; a program needn't handle non-finite values.
Results may differ from a plain program's by a relative error of at most 0.0073.
Values may be sent and summed in bfloat16 or wider, within the bound.
A program may use at most 128 MiB of HBM per device.

v0:
```python
import jax
import jax.numpy as jnp
from jax import lax
from jax.sharding import PartitionSpec as P

M = 1024
ITERS = 2


def with_halo(x, sides, width):
    for axis, dim in sides:
        peers, length = (lax.axis_size(axis), x.shape[dim])
        up = [(i, (i + 1) % peers) for i in range(peers)]
        down = [(j, i) for i, j in up]
        last = lax.slice_in_dim(x, length - width, length, axis=dim)
        first = lax.slice_in_dim(x, 0, width, axis=dim)
        before = lax.ppermute(last, axis, up)
        after = lax.ppermute(first, axis, down)
        x = jnp.concatenate([before, x, after], axis=dim)
    return x


def per_device(ensemble, right_side, obs_prec, neighbors, loc_weight):
    blocks = right_side.shape[0]
    cells = right_side.shape[1]
    total = blocks * lax.axis_size(("mem", "grid"))
    scale = 1.0 / M
    n_mem = lax.axis_size("mem")
    n_grid = lax.axis_size("grid")
    sectioned = ensemble.reshape(ensemble.shape[0], n_mem, n_grid, blocks, cells)
    moved = lax.all_to_all(
        lax.all_to_all(sectioned, "mem", split_axis=1, concat_axis=0, tiled=True),
        "grid",
        split_axis=2,
        concat_axis=0,
        tiled=True,
    )
    relaid = moved.reshape(M, blocks, cells)
    index = lax.axis_index(("mem", "grid"))
    own_nbr = lax.dynamic_slice_in_dim(neighbors, index * blocks, blocks, 0)
    own_weight = lax.dynamic_slice_in_dim(loc_weight, index * blocks, blocks, 0)
    position = (own_nbr - (index - 1) * blocks) % total
    window = jnp.arange(3 * blocks, dtype=jnp.int32)
    mixing = jnp.sum(
        jnp.where(position[:, :, None] == window[None, None, :], own_weight[:, :, None], 0.0),
        axis=1,
    )
    itself = window[None, :] == (blocks + jnp.arange(blocks, dtype=jnp.int32))[:, None]
    mixing = mixing + itself.astype(jnp.float32)
    solution_field = jnp.zeros_like(right_side)
    residual = right_side
    direction = right_side

    def squares(field):
        return lax.psum(jnp.sum(field * field), ("mem", "grid"))

    norm_now = squares(residual)
    for step in range(ITERS):
        rounded = direction.astype(jnp.bfloat16)
        sums = jnp.einsum("mbc,bc->bm", relaid, rounded, preferred_element_type=jnp.float32)
        wider = with_halo(sums, ((("mem", "grid"), 0),), blocks)
        coeff = jnp.dot(
            mixing, wider, precision=lax.Precision.HIGHEST, preferred_element_type=jnp.float32
        ).astype(jnp.bfloat16)
        spread = jnp.einsum("mbc,bm->bc", relaid, coeff, preferred_element_type=jnp.float32)
        image = obs_prec * direction + spread * scale
        alpha = norm_now / lax.psum(jnp.sum(direction * image), ("mem", "grid"))
        solution_field = solution_field + alpha * direction
        residual = residual - alpha * image
        if step + 1 < ITERS:
            norm_next = squares(residual)
            direction = residual + norm_next / norm_now * direction
            norm_now = norm_next
    return (solution_field, residual)


def solution(mesh):
    return jax.shard_map(
        per_device,
        mesh=mesh,
        in_specs=(
            P(("mem", "grid"), None, None),
            P(("mem", "grid"), None),
            P(("mem", "grid"), None),
            P(),
            P(),
        ),
        out_specs=(P(("mem", "grid"), None), P(("mem", "grid"), None)),
        check_vma=False,
    )
```

profile of v0, /device:TPU:1, one launch (start us, length us, event | category | flops | bytes accessed | tf_op | source)
XLA Modules:
  0.0 605.1 jit_solution(232004692093197388)
XLA Ops:
  0.6 10.1 %copy.25 = bf16[4,1024,1024]{2,0,1:T(4,128)(2,1)S(1)} copy(bf16[4,1024,1024]{2,1,0:T(8,128)(2,1)} %param.5) | data formatting | bytes 16777216 | tf_op args[0]
  10.8 101.6 %all_to_all.33 = bf16[4,8,32,4,1024]{4,0,3,2,1:T(4,128)(2,1)} all-to-all(bf16[4,8,32,4,1024]{4,0,3,2,1:T(4,128)(2,1)S(1)} %bitcast.51), channel_id=1, replica_groups=mesh['mem'=8,'grid'=32] {'mem'}, dimensions={1} | all-to-all | bytes 16777216 | tf_op jit(solution)/shard_map/all_to_all | solution.py:32
  112.4 11.7 %copy.26 = bf16[8,4,1,32,4,1024]{5,3,4,2,1,0:T(8,128)(2,1)} copy(bf16[8,4,1,32,4,1024]{5,1,4,3,0,2:T(4,128)(2,1)} %bitcast.49) | data formatting | bytes 16777216 | tf_op jit(solution)/shard_map/all_to_all | solution.py:32
  124.1 12.1 %copy.27 = bf16[32,1,32,4,1024]{4,3,1,0,2:T(4,128)(2,1)} copy(bf16[32,1,32,4,1024]{4,2,3,1,0:T(8,128)(2,1)} %bitcast.50) | data formatting | bytes 16777216 | tf_op jit(solution)/shard_map/all_to_all | solution.py:32
  136.2 12.6 %all-to-all-start.1 = ((bf16[32,1,32,4,1024]{4,3,1,0,2:T(4,128)(2,1)}), bf16[32,1,32,4,1024]{4,3,1,0,2:T(4,128)(2,1)}, u32[]{:S(2)}, u32[]{:S(2)}) async-start(bf16[32,1,32,4,1024]{4,3,1,0,2:T(4,128)(2,1)} %copy.27), calls=%async_computation.1 | async-start | bytes 16777216 | tf_op jit(solution)/shard_map/all_to_all | solution.py:31
  149.1 0.8 add_select_fusion
  150.0 185.5 %all-to-all-done.1 = bf16[32,1,32,4,1024]{4,3,1,0,2:T(4,128)(2,1)} async-done(((bf16[32,1,32,4,1024]{4,3,1,0,2:T(4,128)(2,1)}), bf16[32,1,32,4,1024]{4,3,1,0,2:T(4,128)(2,1)}, u32[]{:S(2)}, u32[]{:S(2)}) %all-to-all-start.1) | async-done | bytes 8388640 | tf_op jit(solution)/shard_map/all_to_all | solution.py:31
  335.5 9.4 %copy.28 = bf16[32,1,32,4,1024]{4,0,2,3,1:T(8,128)(2,1)} copy(bf16[32,1,32,4,1024]{4,3,1,0,2:T(4,128)(2,1)} %all-to-all-done.1) | data formatting | bytes 16777216 | tf_op jit(solution)/shard_map/all_to_all | solution.py:31
  344.9 5.8 fusion.20
  351.2 1.3 collective-permute-start
  352.5 1.4 collective-permute-done.1
  354.2 1.2 fusion.18
  355.4 0.6 multiply_reduce_fusion.2
  356.0 76.5 %all-reduce = (f32[]{:T(128)}, f32[]{:T(128)}) all-reduce(f32[]{:T(128)} %get-tuple-element.3, f32[]{:T(128)} %get-tuple-element.2), channel_id=1, replica_groups=mesh['mem'=8,'grid'=32] {'mem','grid'}, use_global_device_ids=true, to_apply=%region_1.2 | all-reduce | flops 2 | bytes 16 | tf_op jit(solution)/shard_map/psum | solution.py:55
  433.8 0.6 multiply_reduce_fusion.1
  434.4 74.5 %psum.30 = f32[]{:T(128)} all-reduce(f32[]{:T(128)} %get-tuple-element.6), channel_id=1, replica_groups=mesh['mem'=8,'grid'=32] {'mem','grid'}, use_global_device_ids=true, to_apply=%region_6.7 | all-reduce | flops 1 | bytes 8 | tf_op jit(solution)/shard_map/psum | solution.py:55
  510.2 5.6 fusion.16
  515.9 0.7 collective-permute-start.3
  516.6 1.1 collective-permute-start.2
  517.6 1.4 collective-permute-done.3
  519.6 4.6 fusion.14
  524.2 0.6 multiply_reduce_fusion
  524.8 78.4 %psum.31 = f32[]{:T(128)} all-reduce(f32[]{:T(128)} %multiply_reduce_fusion), channel_id=1, replica_groups=mesh['mem'=8,'grid'=32] {'mem','grid'}, use_global_device_ids=true, to_apply=%region_8.9 | all-reduce | flops 1 | bytes 8 | tf_op jit(solution)/shard_map/psum | solution.py:67
  604.5 0.6 multiply_subtract_fusion
  (22 shorter events, 1.7 us)
Async XLA Ops:
  0.6 148.2 %copy-start = (f32[1024,8]{0,1:T(8,128)S(1)}, f32[1024,8]{0,1:T(8,128)}, u32[]{:S(2)}) copy-start(f32[1024,8]{0,1:T(8,128)} %param.9) | copy-start | bytes 98308
  136.2 13.8 %copy-start.2 = (f32[4,1024]{1,0:T(4,128)S(1)}, f32[4,1024]{1,0:T(4,128)}, u32[]{:S(2)}) copy-start(f32[4,1024]{1,0:T(4,128)} %param.6) | copy-start | bytes 49156
  136.2 199.2 %all-to-all-start.1 = ((bf16[32,1,32,4,1024]{4,3,1,0,2:T(4,128)(2,1)}), bf16[32,1,32,4,1024]{4,3,1,0,2:T(4,128)(2,1)}, u32[]{:S(2)}, u32[]{:S(2)}) async-start(bf16[32,1,32,4,1024]{4,3,1,0,2:T(4,128)(2,1)} %copy.27), calls=%async_computation.1 | async-start | bytes 16777216 | tf_op jit(solution)/shard_map/all_to_all | solution.py:31
  344.9 9.2 %copy-start.1 = (bf16[32,1,32,4,1024]{4,0,2,3,1:T(8,128)(2,1)S(1)}, bf16[32,1,32,4,1024]{4,0,2,3,1:T(8,128)(2,1)}, u32[]{:S(2)}) copy-start(bf16[32,1,32,4,1024]{4,0,2,3,1:T(8,128)(2,1)} %copy.28) | copy-start | bytes 25165828
  344.9 10.4 %copy-start.3 = (f32[4,1024]{1,0:T(4,128)S(1)}, f32[4,1024]{1,0:T(4,128)}, u32[]{:S(2)}) copy-start(f32[4,1024]{1,0:T(4,128)} %param.7) | copy-start | bytes 49156
  350.7 3.2 collective-permute-start.1
  351.2 2.7 collective-permute-start
  515.9 3.2 collective-permute-start.3
  516.6 2.8 collective-permute-start.2
where the time goes:
time: 606 us; the launch traced here: 605 us
  blocking collectives  331 us (55%)
  waiting for transfers between devices  189 us (31%)
  local copies, waits for them, and re-layouts  43.7 us (7%)
  matrix products  17.7 us (3%)
  starting transfers between devices  16.2 us (3%)
    all_to_all x1, waiting for transfers between devices, per_device(): lax.all_to_all(lax.all_to_all(sectioned, 'mem', split_axis=1, concat_axis...  185 us
    psum x2, blocking collectives, squares(): return lax.psum(jnp.sum(field * field), ('mem', 'grid'))  151 us
    all_to_all x1, blocking collectives, per_device(): lax.all_to_all(sectioned, 'mem', split_axis=1, concat_axis=0, tiled=True)  102 us
    psum x1, blocking collectives, per_device(): alpha = norm_now / lax.psum(jnp.sum(direction * image), ('mem', 'grid'))  78.4 us
    all_to_all x2, local copies, waits for them, and re-layouts, per_device(): lax.all_to_all(sectioned, 'mem', split_axis=1, concat_axis=0, tiled=True)  23.8 us
    all_to_all x1, starting transfers between devices, per_device(): lax.all_to_all(lax.all_to_all(sectioned, 'mem', split_axis=1, concat_axis...  12.6 us
  transfers between devices with their start and end apart: 5, of which 4 were waited for; matrix products, arithmetic and copies ran while one was open for 0% of the time, Pallas kernels for 0%

commit v1 on v0

v1 whole, which is shorter than its diff:
```python
import functools

import jax
import jax.numpy as jnp
from jax import lax
from jax.experimental import pallas as pl
from jax.experimental.pallas import tpu as pltpu
from jax.sharding import PartitionSpec as P

M = 1024
ITERS = 2
NX, NY, NZ = 4, 4, 8
LANE = 128
F32, BF16 = jnp.float32, jnp.bfloat16
MESH = pl.DeviceIdType.MESH


def kernel(
    ens, rhs, obs, nbr, wgt, sol_out, res_out,
    half, gath, part, from_r1, line_t, from_r2, line_u, from_r3, whole, from_sib,
    high, low, expand, sums, sums_sib, sums_prev, mix, coeff_t, onehot, select,
    field, stat, stat_in,
    ens_sem, ens_send, ens_recv,
    s0, r0s, s1, r1s, s2, r2s, s3, r3s,
    t1, u1, t2, u2, t3, u3, t4, u4, bs_s, bs_r, st_s, st_r,
):
    mem, grid = lax.axis_index("mem"), lax.axis_index("grid")
    y, z, core = mem % NY, grid // 4, grid % 2
    x = (mem // NY) * 2 + (grid // 2) % 2
    other = 1 - core
    first = core == 0

    def device(xx, yy, zz, cc):
        return ((xx // 2) * NY + yy, zz * 4 + (xx % 2) * 2 + cc)

    sibling = device(x, y, z, other)

    def x_of(d):
        return (x + d) % NX

    def y_of(d):
        return (y + d) % NY

    def z_of(d):
        return (z + d) % NZ

    partners = [sibling]
    partners += [device(x, y, z_of(d), core) for d in range(1, NZ)]
    partners += [device(x_of(d), y, z, core) for d in range(1, NX)]
    partners += [device(x, y_of(d), z, core) for d in range(1, NY)]

    barrier = pltpu.get_barrier_semaphore()
    for there in partners:
        pl.semaphore_signal(barrier, inc=1, device_id=there, device_id_type=MESH)

    def remote(src, dst, send, recv, there):
        return pltpu.make_async_remote_copy(
            src_ref=src, dst_ref=dst, send_sem=send, recv_sem=recv,
            device_id=there, device_id_type=MESH,
        )

    res, direc, prec, answer = (field.at[i] for i in range(4))
    for g in range(8):
        cols = pl.ds(g * LANE, LANE)
        res[pl.ds(4 * g, 4), :] = rhs[:, cols]
        prec[pl.ds(4 * g, 4), :] = obs[:, cols]
    direc[...] = jnp.zeros_like(direc)
    answer[...] = jnp.zeros_like(answer)
    sums_prev[...] = jnp.zeros_like(sums_prev)

    lanes = lax.broadcasted_iota(jnp.int32, (8, M), 1)
    rows = lax.broadcasted_iota(jnp.int32, (8, M), 0)
    onehot[...] = jnp.where(lanes // LANE == rows, 1.0, 0.0).astype(BF16)
    big_lane = lax.broadcasted_iota(jnp.int32, (LANE, M), 1)
    big_row = lax.broadcasted_iota(jnp.int32, (LANE, M), 0)
    select[...] = jnp.where(big_lane // LANE == big_row, 1.0, 0.0).astype(BF16)
    coeff_t[...] = jnp.zeros_like(coeff_t)

    upper = lax.broadcasted_iota(jnp.int32, (8, LANE), 0) < 4

    def total(v):
        return jnp.broadcast_to(jnp.sum(v, axis=(0, 1), keepdims=True), (8, LANE))

    def line(ref, it, xx, yy):
        return ref.at[it, xx // 2, yy, :, xx % 2]

    own_rows = pl.ds(pl.multiple_of(core * 16, 16), 16)
    sib_rows = pl.ds(pl.multiple_of(other * 16, 16), 16)

    pl.semaphore_wait(barrier, len(partners))

    def members(k):
        mine = ens.at[k, :, pl.ds(pl.multiple_of(core * 512, 512), 512)]
        theirs = ens.at[k, :, pl.ds(pl.multiple_of(other * 512, 512), 512)]
        slot = half.at[core * 4 + k]
        return (
            pltpu.make_async_copy(mine, slot, ens_sem.at[k]),
            remote(theirs, slot, ens_send.at[k], ens_recv.at[k], sibling),
        )

    def iteration(it, rr_prev):
        held = []

        def send(*args):
            copy = remote(*args)
            copy.start()
            held.append(copy)
            return copy

        def exchange(kind, value, theres):
            stat[it, kind] = value
            copies = [
                send(stat.at[it, kind], stat_in.at[it, kind, i], st_s.at[it, kind, i], st_r.at[it, kind, i], there)
                for i, there in enumerate(theres)
            ]

            def finish():
                out = value
                for i, copy in enumerate(copies):
                    copy.wait_recv()
                for i in range(len(copies)):
                    out = out + stat_in[it, kind, i]
                return out

            return finish

        z_line = [device(x, y, z_of(d), core) for d in range(1, NZ)]
        x_line = [device(x_of(d), y, z, core) for d in range(1, NX)]
        y_line = [device(x, y_of(d), z, core) for d in range(1, NY)]

        packed = field.at[4 + it]
        r = res[...]
        packed_b = whole.at[it]
        packed_b[...] = r.astype(BF16)
        mine = gath.at[it, x // 2, y, z, x % 2]
        c0 = send(packed_b.at[sib_rows], mine.at[own_rows], s0.at[it], r0s.at[it], sibling)
        rr_fin = exchange(0, total(r * r), [sibling])
        mine[own_rows, :] = packed_b[own_rows, :]
        c0.wait_recv()

        c1 = [
            send(mine, mine, s1.at[it, i], r1s.at[it, i], there)
            for i, there in enumerate(z_line)
        ]
        rr_fin = exchange(1, rr_fin(), z_line)
        return_first = None

        @pl.when(it == 0)
        def _():
            for k in range(4):
                for copy in members(k):
                    copy.start()
            rel = nbr[...] - lanes + 3
            rel = jnp.where(rel < 0, rel + M, rel)
            rel = jnp.where(rel >= M, rel - M, rel)
            w = wgt[...]
            for o in range(7):
                row = jnp.sum(jnp.where(rel == o, w, 0.0), axis=0, keepdims=True)
                mix[pl.ds(o, 1), :] = row + (1.0 if o == 3 else 0.0)

        for copy in c1:
            copy.wait_recv()

        own_line = line(gath, it, x, y)
        c2 = [
            send(own_line, own_line, s2.at[it, i], r2s.at[it, i], there)
            for i, there in enumerate(x_line + y_line)
        ]
        rr_fin = exchange(2, rr_fin(), x_line)

        def hop3(a, b):
            sx = jnp.where(first, x_of(a), x)
            sy = jnp.where(first, y, y_of(b))
            there = device(jnp.where(first, x, x_of(a)), jnp.where(first, y_of(b), y), z, core)
            part_line = line(gath, it, sx, sy)
            return remote(part_line, part_line, s3.at[it, a - 1, b - 1], r3s.at[it, a - 1, b - 1], there)

        for i in range(3):
            c2[i].wait_recv()
        for i in range(3):
            c2[3 + i].wait_recv()
        for b in range(1, 4):
            for a in range(1, 4):
                copy = hop3(a, b)
                copy.start()
                held.append(copy)
        rr_fin = exchange(3, rr_fin(), y_line)

        @pl.when(it == 0)
        def _():
            for k in range(4):
                local, away = members(k)
                local.wait()
                away.wait()

        def block_sums(step):
            yy = y_of(4 - step)

            def body(i, carry):
                xh, zz = i // NZ, i % NZ
                row0 = pl.multiple_of(((xh * NY + yy) * NZ + zz) * 16, 16)
                tiles = [[], [], [], []]
                for xl in range(2):
                    ch = gath[it, xh, yy, zz, xl].astype(F32)
                    for j in range(2):
                        a = ch[8 * j : 8 * j + 8]
                        b = ch[16 + 8 * j : 24 + 8 * j]
                        tiles[2 * j].append(jnp.where(upper, a, pltpu.roll(b, 4, 0)))
                        tiles[2 * j + 1].append(jnp.where(upper, pltpu.roll(a, 4, 0), b))
                tiles = [jnp.concatenate(t, axis=0) for t in tiles]
                at = pl.ds(pl.multiple_of(i * 16, 16), 16)
                for k in range(8):
                    e = half[k, pl.ds(row0, 16), :].astype(F32)
                    acc = e[:, 0:LANE] * tiles[0]
                    for g in range(1, 4):
                        acc = acc + e[:, g * LANE : (g + 1) * LANE] * tiles[g]
                    top = acc.astype(BF16)
                    high[at, k * LANE : (k + 1) * LANE] = top
                    low[at, k * LANE : (k + 1) * LANE] = (acc - top.astype(F32)).astype(BF16)
                return carry

            lax.fori_loop(0, 2 * NZ, body, 0)
            dims = (((1,), (1,)), ((), ()))
            for xh in range(2):
                at = pl.ds(xh * LANE, LANE)
                got = lax.dot_general(onehot[...], high[at, :], dims, preferred_element_type=F32)
                got = got + lax.dot_general(onehot[...], low[at, :], dims, preferred_element_type=F32)
                sums[it, xh * NY + yy] = got
                unit = xh * NY + yy
                copy = remote(
                    sums.at[it, unit], sums_sib.at[it, unit],
                    bs_s.at[it, step, xh], bs_r.at[it, step, xh], sibling,
                )
                copy.start()
                held.append(copy)

        sum_copies = len(held)
        block_sums(0)
        for step in range(1, 4):
            b = jnp.where(first, step, 4 - step)
            for a in range(1, 4):
                dummy = line(gath, it, x, y)
                remote(dummy, dummy, s3.at[it, a - 1, b - 1], r3s.at[it, a - 1, b - 1], sibling).wait_recv()
            block_sums(step)
        sum_copies = held[sum_copies:]

        rr = rr_fin()
        beta = jnp.where(it == 0, 0.0, rr / rr_prev)
        p = r + beta[0:1] * direc[...]
        direc[...] = p
        dp = prec[...] * p
        pdp_fin = exchange(4, total(p * dp), [sibling])
        for copy in sum_copies:
            copy.wait_recv()

        bs = [sums[it, u] + sums_sib[it, u] + beta * sums_prev[u] for u in range(8)]
        for u in range(8):
            sums_prev[u] = bs[u]
        bs = jnp.concatenate(bs, axis=1)
        co = mix[3:4, :] * bs
        for o in (0, 1, 2, 4, 5, 6):
            co = co + mix[o : o + 1, :] * pltpu.roll(bs, (3 - o) % M, 1)
        co = co.astype(BF16).astype(F32)
        quad_fin = exchange(5, total(co * bs) * (1.0 / M) + pdp_fin(), y_line)
        for u in range(8):
            coeff_t[u, 0:8, :] = co[:, u * LANE : (u + 1) * LANE]

        def spread(step):
            yy = y_of(4 - step)
            for xh in range(2):
                cols = coeff_t[xh * NY + yy].T.astype(BF16)
                expand[xh] = jnp.dot(cols, select[...], preferred_element_type=F32)

            def body(i, carry):
                xh, zz = i // NZ, i % NZ
                row0 = pl.multiple_of(((xh * NY + yy) * NZ + zz) * 16, 16)
                at = pl.ds(pl.multiple_of(zz * 16, 16), 16)
                acc = [None] * 4
                for k in range(8):
                    e = half[k, pl.ds(row0, 16), :].astype(F32)
                    ck = expand[xh, at, k * LANE : (k + 1) * LANE]
                    for g in range(4):
                        term = e[:, g * LANE : (g + 1) * LANE] * ck
                        acc[g] = term if k == 0 else acc[g] + term
                for xl in range(2):
                    t = [v[8 * xl : 8 * xl + 8] for v in acc]
                    lo = [jnp.where(upper, t[2 * j], pltpu.roll(t[2 * j + 1], 4, 0)) for j in range(2)]
                    hi = [jnp.where(upper, pltpu.roll(t[2 * j], 4, 0), t[2 * j + 1]) for j in range(2)]
                    part[it, xh, yy, zz, xl] = jnp.concatenate(lo + hi, axis=0).astype(BF16)
                return carry

            lax.fori_loop(0, 2 * NZ, body, 0)

        def hop_r1(p_, q):
            lx = jnp.where(first, x_of(q), x_of(p_))
            ly = jnp.where(first, y_of(p_), y_of(q))
            there = device(jnp.where(first, x, x_of(p_)), jnp.where(first, y_of(p_), y), z, core)
            return remote(line(part, it, lx, ly), from_r1.at[it, p_ - 1, q], t1.at[it, p_ - 1, q], u1.at[it, p_ - 1, q], there)

        for step in (1, 2, 3, 0):
            spread(step)
            if step:

                @pl.when(first)
                def _():
                    for q in range(4):
                        hop_r1(4 - step, q).start()

            @pl.when(jnp.logical_not(first))
            def _():
                for p_ in range(1, 4):
                    hop_r1(p_, (4 - step) % 4).start()

        quad_fin = exchange(6, quad_fin(), x_line)

        def own(q):
            return jnp.where(first, x_of(q), x), jnp.where(first, y, y_of(q))

        c5 = []
        for q in (2, 1, 3, 0):
            for p_ in range(1, 4):
                hop_r1(p_, q).wait_recv()
            lx, ly = own(q)

            def add1(zz, carry, q=q, lx=lx, ly=ly):
                v = part[it, lx // 2, ly, zz, lx % 2].astype(F32)
                for p_ in range(3):
                    v = v + from_r1[it, p_, q, zz].astype(F32)
                if q:
                    line_t[it, q - 1, zz] = v.astype(BF16)
                else:
                    line_u[it, zz] = v
                return carry

            lax.fori_loop(0, NZ, add1, 0)
            if q:
                c5.append(send(line_t.at[it, q - 1], from_r2.at[it, q - 1], t2.at[it, q - 1], u2.at[it, q - 1], device(lx, ly, z, core)))
        for copy in c5:
            copy.wait_recv()

        def add2(zz, carry):
            v = line_u[it, zz]
            for q in range(3):
                v = v + from_r2[it, q, zz].astype(F32)
            line_u[it, zz] = v
            return carry

        lax.fori_loop(0, NZ, add2, 0)

        c6 = [
            send(line_u.at[it, z_of(d)], from_r3.at[it, d - 1], t3.at[it, d - 1], u3.at[it, d - 1], device(x, y, z_of(d), core))
            for d in (4, 3, 5, 2, 6, 1, 7)
        ]
        quad_fin = exchange(7, quad_fin(), z_line)
        for copy in c6:
            copy.wait_recv()
        v = line_u[it, z]
        for d in range(7):
            v = v + from_r3[it, d]
        chip = field.at[4 + it]
        chip[...] = v
        c7 = send(chip.at[sib_rows], from_sib.at[it, own_rows], t4.at[it], u4.at[it], sibling)
        from_sib[it, own_rows, :] = chip[own_rows, :]
        alpha = (rr / quad_fin())[0:1]
        answer[...] = answer[...] + alpha * p
        c7.wait_recv()
        image = dp + from_sib[it] * (1.0 / M)
        res[...] = r - alpha * image

        for copy in held:
            copy.wait_send()
        for p_ in range(1, 4):
            for q in range(4):
                hop_r1(p_, q).wait_send()
        return rr

    lax.fori_loop(0, ITERS, iteration, jnp.ones((8, LANE), F32))

    for g in range(8):
        cols = pl.ds(g * LANE, LANE)
        sol_out[:, cols] = answer[pl.ds(4 * g, 4), :]
        res_out[:, cols] = res[pl.ds(4 * g, 4), :]


def per_device(ensemble, right_side, obs_prec, neighbors, loc_weight):
    vmem = pl.BlockSpec(memory_space=pltpu.VMEM)
    dma = lambda *n: pltpu.SemaphoreType.DMA(n)
    out = jax.ShapeDtypeStruct(right_side.shape, F32)
    return pl.pallas_call(
        kernel,
        out_shape=(out, out),
        in_specs=[pl.BlockSpec(memory_space=pl.ANY), vmem, vmem, vmem, vmem],
        out_specs=(vmem, vmem),
        scratch_shapes=[
            pltpu.VMEM((8, M, 512), BF16),
            pltpu.VMEM((2, 2, NY, NZ, 2, 32, LANE), BF16),
            pltpu.VMEM((2, 2, NY, NZ, 2, 32, LANE), BF16),
            pltpu.VMEM((2, 3, 4, NZ, 32, LANE), BF16),
            pltpu.VMEM((2, 3, NZ, 32, LANE), BF16),
            pltpu.VMEM((2, 3, NZ, 32, LANE), BF16),
            pltpu.VMEM((2, NZ, 32, LANE), F32),
            pltpu.VMEM((2, 7, 32, LANE), F32),
            pltpu.VMEM((2, 32, LANE), BF16),
            pltpu.VMEM((2, 32, LANE), F32),
            pltpu.VMEM((256, M), BF16),
            pltpu.VMEM((256, M), BF16),
            pltpu.VMEM((2, LANE, M), F32),
            pltpu.VMEM((2, 8, 8, LANE), F32),
            pltpu.VMEM((2, 8, 8, LANE), F32),
            pltpu.VMEM((8, 8, LANE), F32),
            pltpu.VMEM((8, M), F32),
            pltpu.VMEM((8, LANE, LANE), F32),
            pltpu.VMEM((8, M), BF16),
            pltpu.VMEM((LANE, M), BF16),
            pltpu.VMEM((6, 32, LANE), F32),
            pltpu.VMEM((2, 8, 8, LANE), F32),
            pltpu.VMEM((2, 8, 7, 8, LANE), F32),
            dma(4), dma(4), dma(4),
            dma(2), dma(2), dma(2, 7), dma(2, 7), dma(2, 6), dma(2, 6), dma(2, 3, 3), dma(2, 3, 3),
            dma(2, 3, 4), dma(2, 3, 4), dma(2, 3), dma(2, 3), dma(2, 7), dma(2, 7), dma(2), dma(2),
            dma(2, 4, 2), dma(2, 4, 2), dma(2, 8, 7), dma(2, 8, 7),
        ],
        compiler_params=pltpu.CompilerParams(
            collective_id=0, has_side_effects=True, vmem_limit_bytes=56 * 2**20
        ),
    )(ensemble, right_side, obs_prec, neighbors.T, loc_weight.T)


def solution(mesh):
    return jax.shard_map(
        per_device,
        mesh=mesh,
        in_specs=(
            P(("mem", "grid"), None, None),
            P(("mem", "grid"), None),
            P(("mem", "grid"), None),
            P(),
            P(),
        ),
        out_specs=(P(("mem", "grid"), None), P(("mem", "grid"), None)),
        check_vma=False,
    )
```

time: 606 us -> 111 us (0.18)
  blocking collectives: 331 us -> 0 us
  waiting for transfers between devices: 189 us -> 0 us
  Pallas kernels: 0 us -> 107 us
  local copies, waits for them, and re-layouts: 43.7 us -> 2.65 us
  matrix products: 17.7 us -> 0 us
  starting transfers between devices: 16.2 us -> 0 us
    psum x3 -> x0, blocking collectives: 229 us -> none  [the longest x2 151 us: squares(): return lax.psum(jnp.sum(field * field), ('mem', 'grid'))]
    all_to_all x1 -> x0, waiting for transfers between devices: 185 us -> none  [per_device(): lax.all_to_all(lax.all_to_all(sectioned, 'mem', split_axis=1, concat_axis...]
    pallas_call x0 -> x1, Pallas kernels: none -> 107 us  [per_device(): pl.pallas_call(kernel, out_shape=(out, out), in_specs=[pl.BlockSpec(memor...]
    all_to_all x1 -> x0, blocking collectives: 102 us -> none  [per_device(): lax.all_to_all(sectioned, 'mem', split_axis=1, concat_axis=0, tiled=True)]
    all_to_all x3 -> x0, local copies, waits for them, and re-layouts: 33.3 us -> none  [the longest x2 23.8 us: per_device(): lax.all_to_all(sectioned, 'mem', split_axis=1, concat_axis=0, tiled=True)]
    dot_general x6 -> x0, matrix products: 17.7 us -> none  [the longest x2 11.4 us: per_device(): jnp.einsum('mbc,bc->bm', relaid, rounded, preferred_element_type=jnp.floa...]
    all_to_all x1 -> x0, starting transfers between devices: 12.6 us -> none  [per_device(): lax.all_to_all(lax.all_to_all(sectioned, 'mem', split_axis=1, concat_axis...]
    unnamed x9 -> x2, local copies, waits for them, and re-layouts: 10.1 us -> 2.65 us
  transfers between devices with their start and end apart: 5 -> 0, of which waited for: 4 -> 0; matrix products, arithmetic and copies ran while one was open for 0% -> 0% of each run, Pallas kernels for 0% -> 0%
where the time goes in v1:
time: 111 us
  Pallas kernels  107 us (96%)
  local copies, waits for them, and re-layouts  2.65 us (2%)
    pallas_call x1, Pallas kernels, per_device(): pl.pallas_call(kernel, out_shape=(out, out), in_specs=[pl.BlockSpec(memor...  107 us
    unnamed x2, local copies, waits for them, and re-layouts  2.65 us

profile of v1, /device:TPU:1, one launch (start us, length us, event | category | flops | bytes accessed | tf_op | source)
XLA Modules:
  0.0 110.7 jit_solution(14694833056320699881)
XLA Ops:
  0.6 107.4 %shard_map.68 = (f32[4,1024]{1,0:T(4,128)}, f32[4,1024]{1,0:T(4,128)}) custom-call(bf16[4,1024,1024]{2,1,0:T(8,128)(2,1)} %ens.1, f32[4,1024]{1,0:T(4,128)} %rhs.1, f32[4,1024]{1,0:T(4,128)} %obs.1, s32[8,1024]{1,0:T(8,128)} %bitcast.2, f32[8,1024]{1,0:T(8,128)} %bitcast.3), custom_call_target="tpu_custom_call" | custom-call | tf_op jit(solution)/shard_map/pallas_call | solution.py:389
  108.0 1.3 %copy.9 = f32[4,1024]{1,0:T(4,128)} copy(f32[4,1024]{1,0:T(4,128)} %get-tuple-element.4) | data formatting | bytes 32768
  109.3 1.3 %copy.10 = f32[4,1024]{1,0:T(4,128)} copy(f32[4,1024]{1,0:T(4,128)} %get-tuple-element.5) | data formatting | bytes 32768

commit v2 on v1

v2 whole, which is shorter than its diff:
```python
import functools

import jax
import jax.numpy as jnp
from jax import lax
from jax.experimental import pallas as pl
from jax.experimental.pallas import tpu as pltpu
from jax.sharding import PartitionSpec as P

M = 1024
ITERS = 2
NX, NY, NZ = 4, 4, 8
LANE = 128
F32, BF16 = jnp.float32, jnp.bfloat16
MESH = pl.DeviceIdType.MESH


def kernel(
    ens, rhs, obs, nbr, wgt, out,
    half, gath, part, from_r1, line_t, from_r2, line_u, from_r3, packed, whole,
    high, low, expand, sums, sums_sib, sums_prev, mix, coeff_t, onehot, select,
    field, stat, stat_in, span,
    ens_local, ens_send, ens_recv,
    r1s, r2s, r3s, u1, u2, u3, bs_r, st_r, sends,
):
    mem, grid = lax.axis_index("mem"), lax.axis_index("grid")
    y, z, core = mem % NY, grid // 4, grid % 2
    x = (mem // NY) * 2 + (grid // 2) % 2
    other = 1 - core
    first = core == 0

    def device(xx, yy, zz, cc):
        return ((xx // 2) * NY + yy, zz * 4 + (xx % 2) * 2 + cc)

    sibling = device(x, y, z, other)

    def x_of(d):
        return (x + d) % NX

    def y_of(d):
        return (y + d) % NY

    def z_of(d):
        return (z + d) % NZ

    def fwd(d):
        return device(jnp.where(first, x_of(d), x), jnp.where(first, y, y_of(d)), z, core)

    def cross(d):
        return device(jnp.where(first, x, x_of(d)), jnp.where(first, y_of(d), y), z, core)

    z_steps = [(d, 0) for d in range(1, NZ)] + [(d, 1) for d in range(NZ)]
    z_line = [device(x, y, z_of(d), other if e else core) for d, e in z_steps]
    far_first = sorted(range(15), key=lambda i: -min(z_steps[i][0], NZ - z_steps[i][0]))
    fwd_line = [fwd(d) for d in range(1, 4)]
    cross_line = [cross(d) for d in range(1, 4)]
    partners = z_line + fwd_line + cross_line

    barrier = pltpu.get_barrier_semaphore()
    for there in partners:
        pl.semaphore_signal(barrier, inc=1, device_id=there, device_id_type=MESH)

    def remote(src, dst, send, recv, there):
        return pltpu.make_async_remote_copy(
            src_ref=src, dst_ref=dst, send_sem=send, recv_sem=recv,
            device_id=there, device_id_type=MESH,
        )

    res, direc, prec, answer = (field.at[i] for i in range(4))
    for g in range(8):
        cols = pl.ds(g * LANE, LANE)
        res[pl.ds(4 * g, 4), :] = rhs[:, cols]
        prec[pl.ds(4 * g, 4), :] = obs[:, cols]
    direc[...] = jnp.zeros_like(direc)
    answer[...] = jnp.zeros_like(answer)
    sums_prev[...] = jnp.zeros_like(sums_prev)

    lanes = lax.broadcasted_iota(jnp.int32, (8, M), 1)
    rows = lax.broadcasted_iota(jnp.int32, (8, M), 0)
    onehot[...] = jnp.where(lanes // LANE == rows, 1.0, 0.0).astype(BF16)
    big_lane = lax.broadcasted_iota(jnp.int32, (LANE, M), 1)
    big_row = lax.broadcasted_iota(jnp.int32, (LANE, M), 0)
    select[...] = jnp.where(big_lane // LANE == big_row, 1.0, 0.0).astype(BF16)
    coeff_t[...] = jnp.zeros_like(coeff_t)

    upper = lax.broadcasted_iota(jnp.int32, (8, LANE), 0) < 4

    def total(v):
        return jnp.broadcast_to(jnp.sum(v, axis=(0, 1), keepdims=True), (1, LANE))

    def line(ref, it, xx, yy):
        return ref.at[it, xx // 2, yy, :, xx % 2]

    own_rows = pl.ds(pl.multiple_of(core * 16, 16), 16)
    sib_rows = pl.ds(pl.multiple_of(other * 16, 16), 16)
    mine_four = half.at[pl.ds(pl.multiple_of(core * 4, 4), 4)]
    sib_four = half.at[pl.ds(pl.multiple_of(other * 4, 4), 4)]

    def members_local():
        src = ens.at[:, :, pl.ds(pl.multiple_of(core * 512, 512), 512)]
        return pltpu.make_async_copy(src, mine_four, ens_local)

    def members_away():
        src = ens.at[:, :, pl.ds(pl.multiple_of(other * 512, 512), 512)]
        return remote(src, mine_four, ens_send, ens_recv, sibling)

    members_local().start()
    pl.semaphore_wait(barrier, len(partners))

    def wait_bytes(ref, sem):
        pltpu.make_async_copy(ref, ref, sem).wait()

    def iteration(it, rr_prev):
        def send(src, dst, kind, recv, there):
            remote(src, dst, sends.at[kind], recv, there).start()

        def landed(dst, recv):
            pltpu.make_async_copy(dst, dst, recv).wait()

        def exchange(kind, slot, value, theres):
            stat[it, kind] = value
            for i, there in enumerate(theres):
                send(stat.at[it, kind], stat_in.at[it, slot + i], 5, st_r.at[it, kind], there)

            def finish():
                wait_bytes(stat_in.at[it, pl.ds(slot, len(theres))], st_r.at[it, kind])
                got = value
                for i in range(len(theres)):
                    got = got + stat_in[it, slot + i]
                return got

            return finish

        r = res[...]
        pack = packed.at[it]
        pack[...] = r.astype(BF16)
        mine = gath.at[it, x // 2, y, z, x % 2]
        for i in far_first:
            send(pack.at[sib_rows if z_steps[i][1] else own_rows], mine.at[own_rows], 0, r1s.at[it, i], z_line[i])
        rr_fin = exchange(0, 0, total(r * r), z_line)
        mine[own_rows, :] = pack[own_rows, :]

        @pl.when(it == 0)
        def _():
            members_away().start()
            rel = nbr[...] - lanes + 3
            rel = jnp.where(rel < 0, rel + M, rel)
            rel = jnp.where(rel >= M, rel - M, rel)
            w = wgt[...]
            for o in range(7):
                row = jnp.sum(jnp.where(rel == o, w, 0.0), axis=0, keepdims=True)
                mix[pl.ds(o, 1), :] = row + (1.0 if o == 3 else 0.0)

        for i in range(15):
            landed(mine.at[own_rows], r1s.at[it, i])

        own_line = line(gath, it, x, y)
        for d in (2, 1, 3):
            send(own_line, own_line, 1, r2s.at[it, d - 1], fwd(d))
        rr_fin = exchange(1, 15, rr_fin(), fwd_line)
        for d in (2, 1, 3):
            send(own_line, own_line, 1, r2s.at[it, 2 + d], cross(d))

        for n, a in enumerate((1, 3, 2)):
            landed(own_line, r2s.at[it, a - 1])
            came = line(gath, it, jnp.where(first, x_of(NX - a), x), jnp.where(first, y, y_of(NY - a)))
            for b in (1, 3, 2):
                send(came, came, 1, r3s.at[it, a - 1, b - 1], cross(b))
        rr_fin = exchange(2, 18, rr_fin(), cross_line)
        for b in range(3):
            landed(own_line, r2s.at[it, 3 + b])

        @pl.when(it == 0)
        def _():
            members_local().wait()
            wait_bytes(sib_four, ens_recv)

        def block_sums(step):
            yy = y_of(4 - step)

            def body(i, carry):
                xh, zz = i // NZ, i % NZ
                row0 = pl.multiple_of(((xh * NY + yy) * NZ + zz) * 16, 16)
                tiles = [[], [], [], []]
                for xl in range(2):
                    ch = gath[it, xh, yy, zz, xl].astype(F32)
                    for j in range(2):
                        a = ch[8 * j : 8 * j + 8]
                        b = ch[16 + 8 * j : 24 + 8 * j]
                        tiles[2 * j].append(jnp.where(upper, a, pltpu.roll(b, 4, 0)))
                        tiles[2 * j + 1].append(jnp.where(upper, pltpu.roll(a, 4, 0), b))
                tiles = [jnp.concatenate(t, axis=0) for t in tiles]
                at = pl.ds(pl.multiple_of(i * 16, 16), 16)
                for k in range(8):
                    e = half[k, pl.ds(row0, 16), :].astype(F32)
                    acc = e[:, 0:LANE] * tiles[0]
                    for g in range(1, 4):
                        acc = acc + e[:, g * LANE : (g + 1) * LANE] * tiles[g]
                    top = acc.astype(BF16)
                    high[at, k * LANE : (k + 1) * LANE] = top
                    low[at, k * LANE : (k + 1) * LANE] = (acc - top.astype(F32)).astype(BF16)
                return carry

            lax.fori_loop(0, 2 * NZ, body, 0)
            dims = (((1,), (1,)), ((), ()))
            for xh in range(2):
                at = pl.ds(xh * LANE, LANE)
                got = lax.dot_general(onehot[...], high[at, :], dims, preferred_element_type=F32)
                got = got + lax.dot_general(onehot[...], low[at, :], dims, preferred_element_type=F32)
                sums[it, xh * NY + yy] = got
                unit = xh * NY + yy
                send(sums.at[it, unit], sums_sib.at[it, unit], 4, bs_r.at[it], sibling)

        for step in (0, 1, 3, 2):
            if step:
                for i in range(1, 4):
                    a, b = jnp.where(first, i, step), jnp.where(first, step, i)
                    landed(own_line, r3s.at[it, a - 1, b - 1])
            block_sums(step)

        rr = rr_fin()
        beta = jnp.where(it == 0, 0.0, rr / rr_prev)
        p = r + beta * direc[...]
        direc[...] = p
        dp = prec[...] * p
        pdp = total(p * dp)
        wait_bytes(sums_sib.at[it], bs_r.at[it])

        bs = [sums[it, u] + sums_sib[it, u] + beta * sums_prev[u] for u in range(8)]
        for u in range(8):
            sums_prev[u] = bs[u]
        bs = jnp.concatenate(bs, axis=1)
        co = mix[3:4, :] * bs
        for o in (0, 1, 2, 4, 5, 6):
            co = co + mix[o : o + 1, :] * pltpu.roll(bs, (3 - o) % M, 1)
        co = co.astype(BF16).astype(F32)
        quad_fin = exchange(3, 21, total(co * bs) * (0.5 / M) + pdp, cross_line)
        for u in range(8):
            coeff_t[u, 0:8, :] = co[:, u * LANE : (u + 1) * LANE]

        def spread(step):
            yy = y_of(4 - step)
            for xh in range(2):
                cols = coeff_t[xh * NY + yy].T.astype(BF16)
                expand[xh] = jnp.dot(cols, select[...], preferred_element_type=F32)

            def body(i, carry):
                xh, zz = i // NZ, i % NZ
                row0 = pl.multiple_of(((xh * NY + yy) * NZ + zz) * 16, 16)
                at = pl.ds(pl.multiple_of(zz * 16, 16), 16)
                acc = [None] * 4
                for k in range(8):
                    e = half[k, pl.ds(row0, 16), :].astype(F32)
                    ck = expand[xh, at, k * LANE : (k + 1) * LANE]
                    for g in range(4):
                        term = e[:, g * LANE : (g + 1) * LANE] * ck
                        acc[g] = term if k == 0 else acc[g] + term
                for xl in range(2):
                    t = [v[8 * xl : 8 * xl + 8] for v in acc]
                    lo = [jnp.where(upper, t[2 * j], pltpu.roll(t[2 * j + 1], 4, 0)) for j in range(2)]
                    hi = [jnp.where(upper, pltpu.roll(t[2 * j], 4, 0), t[2 * j + 1]) for j in range(2)]
                    part[it, xh, yy, zz, xl] = jnp.concatenate(lo + hi, axis=0).astype(BF16)
                return carry

            lax.fori_loop(0, 2 * NZ, body, 0)

        def hop_r1(p_, q):
            lx = jnp.where(first, x_of(q), x_of(p_))
            ly = jnp.where(first, y_of(p_), y_of(q))
            there = device(jnp.where(first, x, x_of(p_)), jnp.where(first, y_of(p_), y), z, core)
            return remote(line(part, it, lx, ly), from_r1.at[it, p_ - 1, q], sends.at[2], u1.at[it, p_ - 1, q], there)

        for step in (2, 1, 3, 0):
            spread(step)
            if step:

                @pl.when(first)
                def _():
                    for q in (2, 1, 3, 0):
                        hop_r1(4 - step, q).start()

            @pl.when(jnp.logical_not(first))
            def _():
                for p_ in (2, 1, 3):
                    hop_r1(p_, (4 - step) % 4).start()

        quad_fin = exchange(4, 24, quad_fin(), fwd_line)

        def own(q):
            return jnp.where(first, x_of(q), x), jnp.where(first, y, y_of(q))

        for q in (2, 1, 3, 0):
            for p_ in range(1, 4):
                landed(from_r1.at[it, p_ - 1, q], u1.at[it, p_ - 1, q])
            lx, ly = own(q)

            def add1(zz, carry, q=q, lx=lx, ly=ly):
                v = part[it, lx // 2, ly, zz, lx % 2].astype(F32)
                for p_ in range(3):
                    v = v + from_r1[it, p_, q, zz].astype(F32)
                if q:
                    line_t[it, q - 1, zz] = v.astype(BF16)
                else:
                    line_u[it, zz] = v
                return carry

            lax.fori_loop(0, NZ, add1, 0)
            if q:
                send(line_t.at[it, q - 1], from_r2.at[it, q - 1], 2, u2.at[it, q - 1], device(lx, ly, z, core))
        quad_fin = exchange(5, 27, quad_fin(), z_line)
        for q in range(3):
            landed(from_r2.at[it, q], u2.at[it, q])

        def add2(zz, carry):
            v = line_u[it, zz]
            for q in range(3):
                v = v + from_r2[it, q, zz].astype(F32)
            line_u[it, zz] = v
            return carry

        lax.fori_loop(0, NZ, add2, 0)

        for i in far_first:
            d, e = z_steps[i]
            send(line_u.at[it, z_of(d), sib_rows if e else own_rows], from_r3.at[it, i], 3, u3.at[it], z_line[i])
        answer_rr = rr / quad_fin()
        answer[...] = answer[...] + answer_rr * p
        wait_bytes(from_r3.at[it], u3.at[it])
        v = line_u[it, z, own_rows, :]
        for i in range(7):
            v = v + from_r3[it, i]
        whole[own_rows, :] = v
        v = from_r3[it, 7]
        for i in range(8, 15):
            v = v + from_r3[it, i]
        whole[sib_rows, :] = v
        res[...] = r - answer_rr * (dp + whole[...] * (1.0 / M))

        wait_bytes(span.at[0:240], sends.at[0])
        wait_bytes(half.at[0, 0:960], sends.at[1])
        wait_bytes(half.at[0, 0:960], sends.at[2])
        wait_bytes(from_r3.at[it], sends.at[3])
        wait_bytes(sums_sib.at[it], sends.at[4])
        wait_bytes(stat_in.at[it], sends.at[5])
        return rr

    lax.fori_loop(0, ITERS, iteration, jnp.ones((1, LANE), F32))
    wait_bytes(mine_four, ens_send)

    for g in range(8):
        cols = pl.ds(g * LANE, LANE)
        out[0:4, cols] = answer[pl.ds(4 * g, 4), :]
        out[4:8, cols] = res[pl.ds(4 * g, 4), :]


def per_device(ensemble, right_side, obs_prec, neighbors, loc_weight):
    vmem = pl.BlockSpec(memory_space=pltpu.VMEM)
    dma = lambda *n: pltpu.SemaphoreType.DMA(n)
    both = pl.pallas_call(
        kernel,
        out_shape=jax.ShapeDtypeStruct((8, M), F32),
        in_specs=[pl.BlockSpec(memory_space=pl.ANY), vmem, vmem, vmem, vmem],
        out_specs=vmem,
        scratch_shapes=[
            pltpu.VMEM((8, M, 512), BF16),
            pltpu.VMEM((2, 2, NY, NZ, 2, 32, LANE), BF16),
            pltpu.VMEM((2, 2, NY, NZ, 2, 32, LANE), BF16),
            pltpu.VMEM((2, 3, 4, NZ, 32, LANE), BF16),
            pltpu.VMEM((2, 3, NZ, 32, LANE), BF16),
            pltpu.VMEM((2, 3, NZ, 32, LANE), BF16),
            pltpu.VMEM((2, NZ, 32, LANE), F32),
            pltpu.VMEM((2, 15, 16, LANE), F32),
            pltpu.VMEM((2, 32, LANE), BF16),
            pltpu.VMEM((32, LANE), F32),
            pltpu.VMEM((256, M), BF16),
            pltpu.VMEM((256, M), BF16),
            pltpu.VMEM((2, LANE, M), F32),
            pltpu.VMEM((2, 8, 8, LANE), F32),
            pltpu.VMEM((2, 8, 8, LANE), F32),
            pltpu.VMEM((8, 8, LANE), F32),
            pltpu.VMEM((8, M), F32),
            pltpu.VMEM((8, LANE, LANE), F32),
            pltpu.VMEM((8, M), BF16),
            pltpu.VMEM((LANE, M), BF16),
            pltpu.VMEM((4, 32, LANE), F32),
            pltpu.VMEM((2, 6, 1, LANE), F32),
            pltpu.VMEM((2, 42, 1, LANE), F32),
            pltpu.VMEM((240, LANE), BF16),
            pltpu.SemaphoreType.DMA, pltpu.SemaphoreType.DMA, pltpu.SemaphoreType.DMA,
            dma(2, 15), dma(2, 6), dma(2, 3, 3), dma(2, 3, 4), dma(2, 3), dma(2), dma(2), dma(2, 6), dma(6),
        ],
        compiler_params=pltpu.CompilerParams(
            collective_id=0, has_side_effects=True, vmem_limit_bytes=56 * 2**20
        ),
    )(ensemble, right_side, obs_prec, neighbors.T, loc_weight.T)
    return both[:4], both[4:]


def solution(mesh):
    return jax.shard_map(
        per_device,
        mesh=mesh,
        in_specs=(
            P(("mem", "grid"), None, None),
            P(("mem", "grid"), None),
            P(("mem", "grid"), None),
            P(),
            P(),
        ),
        out_specs=(P(("mem", "grid"), None), P(("mem", "grid"), None)),
        check_vma=False,
    )
```

time: 111 us -> 94.2 us (0.85)
  Pallas kernels: 107 us -> 91.9 us
  local copies, waits for them, and re-layouts: 2.65 us -> 1.45 us
    pallas_call x1, Pallas kernels: 107 us -> 91.9 us  [per_device(): pl.pallas_call(kernel, out_shape=jax.ShapeDtypeStruct((8, M), F32), in_sp...]
    unnamed x2 -> x0, local copies, waits for them, and re-layouts: 2.65 us -> none
    slice x0 -> x1, local copies, waits for them, and re-layouts: none -> 1.45 us  [per_device(): return (both[:4], both[4:])]
where the time goes in v2:
time: 94.2 us; the launch traced here: 94 us
  Pallas kernels  91.9 us (98%)
  local copies, waits for them, and re-layouts  1.45 us (2%)
    pallas_call x1, Pallas kernels, per_device(): pl.pallas_call(kernel, out_shape=jax.ShapeDtypeStruct((8, M), F32), in_sp...  91.9 us

profile of v2, /device:TPU:1, one launch (start us, length us, event | category | flops | bytes accessed | tf_op | source)
XLA Modules:
  0.0 94.0 jit_solution(15137189726849359661)
XLA Ops:
  0.6 91.9 %shard_map.68 = f32[8,1024]{1,0:T(8,128)} custom-call(bf16[4,1024,1024]{2,1,0:T(8,128)(2,1)} %ens.1, f32[4,1024]{1,0:T(4,128)} %rhs.1, f32[4,1024]{1,0:T(4,128)} %obs.1, s32[8,1024]{1,0:T(8,128)} %bitcast.2, f32[8,1024]{1,0:T(8,128)} %bitcast.3), custom_call_target="tpu_custom_call" | custom-call | tf_op jit(solution)/shard_map/pallas_call | solution.py:359
  92.6 1.5 %fusion = (f32[4,1024]{1,0:T(4,128)}, f32[4,1024]{1,0:T(4,128)}) fusion(f32[8,1024]{1,0:T(8,128)} %shard_map.68), kind=kLoop, calls=%fused_computation | loop fusion | bytes 65536 | tf_op jit(solution)/shard_map/slice | solution.py:396

commit v3 on v2

--- a/solution.py
+++ b/solution.py
@@ -54,7 +54,12 @@
     far_first = sorted(range(15), key=lambda i: -min(z_steps[i][0], NZ - z_steps[i][0]))
     fwd_line = [fwd(d) for d in range(1, 4)]
     cross_line = [cross(d) for d in range(1, 4)]
-    partners = z_line + fwd_line + cross_line
+    near = [(1, 1), (1, 3), (3, 1), (3, 3)]
+
+    def diagonal(a, b):
+        return device(jnp.where(first, x_of(a), x_of(b)), jnp.where(first, y_of(b), y_of(a)), z, core)
+
+    partners = z_line + fwd_line + cross_line + [diagonal(a, b) for a, b in near]
 
     barrier = pltpu.get_barrier_semaphore()
     for there in partners:
@@ -135,8 +140,8 @@
         pack = packed.at[it]
         pack[...] = r.astype(BF16)
         mine = gath.at[it, x // 2, y, z, x % 2]
-        for i in far_first:
-            send(pack.at[sib_rows if z_steps[i][1] else own_rows], mine.at[own_rows], 0, r1s.at[it, i], z_line[i])
+        for i in far_first[::-1]:
+            send(pack.at[sib_rows if z_steps[i][1] else own_rows], mine.at[own_rows], 0, r1s.at[it, z_steps[i][0]], z_line[i])
         rr_fin = exchange(0, 0, total(r * r), z_line)
         mine[own_rows, :] = pack[own_rows, :]
 
@@ -151,22 +156,25 @@
                 row = jnp.sum(jnp.where(rel == o, w, 0.0), axis=0, keepdims=True)
                 mix[pl.ds(o, 1), :] = row + (1.0 if o == 3 else 0.0)
 
-        for i in range(15):
-            landed(mine.at[own_rows], r1s.at[it, i])
-
         own_line = line(gath, it, x, y)
-        for d in (2, 1, 3):
-            send(own_line, own_line, 1, r2s.at[it, d - 1], fwd(d))
+        for d in (0, 1, 7, 2, 6, 3, 5, 4):
+            chunk = own_line.at[z_of(NZ - d)]
+            landed(chunk if d else chunk.at[sib_rows], r1s.at[it, d])
+            for n in (2, 1, 3):
+                send(chunk, chunk, 1, r2s.at[it, n - 1], fwd(n))
         rr_fin = exchange(1, 15, rr_fin(), fwd_line)
         for d in (2, 1, 3):
             send(own_line, own_line, 1, r2s.at[it, 2 + d], cross(d))
-
-        for n, a in enumerate((1, 3, 2)):
+        for a, b in near:
+            send(own_line, own_line, 1, r3s.at[it, jnp.where(first, b, a) - 1], diagonal(a, b))
+
+        rr_fin = exchange(2, 18, rr_fin(), cross_line)
+        for a in (1, 3, 2):
             landed(own_line, r2s.at[it, a - 1])
+        for i, t in ((2, 1), (2, 3), (1, 2), (3, 2), (2, 2)):
+            a, b = jnp.where(first, i, t), jnp.where(first, t, i)
             came = line(gath, it, jnp.where(first, x_of(NX - a), x), jnp.where(first, y, y_of(NY - a)))
-            for b in (1, 3, 2):
-                send(came, came, 1, r3s.at[it, a - 1, b - 1], cross(b))
-        rr_fin = exchange(2, 18, rr_fin(), cross_line)
+            send(came, came, 1, r3s.at[it, t - 1], cross(b))
         for b in range(3):
             landed(own_line, r2s.at[it, 3 + b])
 
@@ -213,9 +221,7 @@
 
         for step in (0, 1, 3, 2):
             if step:
-                for i in range(1, 4):
-                    a, b = jnp.where(first, i, step), jnp.where(first, step, i)
-                    landed(own_line, r3s.at[it, a - 1, b - 1])
+                wait_bytes(from_r1.at[it, 0:3], r3s.at[it, step - 1])
             block_sums(step)
 
         rr = rr_fin()
@@ -238,20 +244,18 @@
         for u in range(8):
             coeff_t[u, 0:8, :] = co[:, u * LANE : (u + 1) * LANE]
 
-        def spread(step):
+        def spread(step, xh):
             yy = y_of(4 - step)
-            for xh in range(2):
-                cols = coeff_t[xh * NY + yy].T.astype(BF16)
-                expand[xh] = jnp.dot(cols, select[...], preferred_element_type=F32)
-
-            def body(i, carry):
-                xh, zz = i // NZ, i % NZ
+            cols = coeff_t[xh * NY + yy].T.astype(BF16)
+            expand[...] = jnp.dot(cols, select[...], preferred_element_type=F32)
+
+            def body(zz, carry):
                 row0 = pl.multiple_of(((xh * NY + yy) * NZ + zz) * 16, 16)
                 at = pl.ds(pl.multiple_of(zz * 16, 16), 16)
                 acc = [None] * 4
                 for k in range(8):
                     e = half[k, pl.ds(row0, 16), :].astype(F32)
-                    ck = expand[xh, at, k * LANE : (k + 1) * LANE]
+                    ck = expand[at, k * LANE : (k + 1) * LANE]
                     for g in range(4):
                         term = e[:, g * LANE : (g + 1) * LANE] * ck
                         acc[g] = term if k == 0 else acc[g] + term
@@ -262,69 +266,66 @@
                     part[it, xh, yy, zz, xl] = jnp.concatenate(lo + hi, axis=0).astype(BF16)
                 return carry
 
-            lax.fori_loop(0, 2 * NZ, body, 0)
-
-        def hop_r1(p_, q):
-            lx = jnp.where(first, x_of(q), x_of(p_))
-            ly = jnp.where(first, y_of(p_), y_of(q))
-            there = device(jnp.where(first, x, x_of(p_)), jnp.where(first, y_of(p_), y), z, core)
-            return remote(line(part, it, lx, ly), from_r1.at[it, p_ - 1, q], sends.at[2], u1.at[it, p_ - 1, q], there)
+            lax.fori_loop(0, NZ, body, 0)
+
+        def line_at(ref, q, p_):
+            return line(ref, it, jnp.where(first, x_of(q), x_of(p_)), jnp.where(first, y_of(p_), y_of(q)))
+
+        def hop_r1(q, p_):
+            slot = 3 * ((q + 3) % 4) + p_ - 1
+            send(line_at(part, q, p_), from_r1.at[it, slot], 2, u1.at[it, 0 if q else 1], cross(p_))
 
         for step in (2, 1, 3, 0):
-            spread(step)
+            for xh in range(2):
+                spread(step, xh)
+
             if step:
 
                 @pl.when(first)
                 def _():
                     for q in (2, 1, 3, 0):
-                        hop_r1(4 - step, q).start()
+                        hop_r1(q, 4 - step)
 
             @pl.when(jnp.logical_not(first))
             def _():
                 for p_ in (2, 1, 3):
-                    hop_r1(p_, (4 - step) % 4).start()
+                    hop_r1((4 - step) % 4, p_)
 
         quad_fin = exchange(4, 24, quad_fin(), fwd_line)
 
-        def own(q):
-            return jnp.where(first, x_of(q), x), jnp.where(first, y, y_of(q))
-
-        for q in (2, 1, 3, 0):
-            for p_ in range(1, 4):
-                landed(from_r1.at[it, p_ - 1, q], u1.at[it, p_ - 1, q])
-            lx, ly = own(q)
-
-            def add1(zz, carry, q=q, lx=lx, ly=ly):
-                v = part[it, lx // 2, ly, zz, lx % 2].astype(F32)
+        wait_bytes(from_r1.at[it, 0:9], u1.at[it, 0])
+
+        def add1(i, carry):
+            d = jnp.where(i % 2 == 1, 4 - (i + 1) // 2, 4 + i // 2)
+            zz = z_of(d)
+            for q in (2, 1, 3):
+                v = line_at(part, q, 0)[zz].astype(F32)
                 for p_ in range(3):
-                    v = v + from_r1[it, p_, q, zz].astype(F32)
-                if q:
-                    line_t[it, q - 1, zz] = v.astype(BF16)
-                else:
-                    line_u[it, zz] = v
-                return carry
-
-            lax.fori_loop(0, NZ, add1, 0)
-            if q:
-                send(line_t.at[it, q - 1], from_r2.at[it, q - 1], 2, u2.at[it, q - 1], device(lx, ly, z, core))
+                    v = v + from_r1[it, 3 * (q - 1) + p_, zz].astype(F32)
+                line_t[it, q - 1, zz] = v.astype(BF16)
+                send(line_t.at[it, q - 1, zz], from_r2.at[it, d, q - 1], 2, u2.at[it, d], fwd(q))
+            return carry
+
+        lax.fori_loop(0, NZ, add1, 0)
         quad_fin = exchange(5, 27, quad_fin(), z_line)
-        for q in range(3):
-            landed(from_r2.at[it, q], u2.at[it, q])
-
-        def add2(zz, carry):
-            v = line_u[it, zz]
+        wait_bytes(from_r1.at[it, 9:12], u1.at[it, 1])
+
+        own_part = line(part, it, x, y)
+        for d in (4, 3, 5, 2, 6, 1, 7, 0):
+            zz = z_of(d)
+            wait_bytes(from_r2.at[it, d], u2.at[it, d])
+            v = own_part[zz].astype(F32)
+            for p_ in range(3):
+                v = v + from_r1[it, 9 + p_, zz].astype(F32)
             for q in range(3):
-                v = v + from_r2[it, q, zz].astype(F32)
+                v = v + from_r2[it, d, q].astype(F32)
             line_u[it, zz] = v
-            return carry
-
-        lax.fori_loop(0, NZ, add2, 0)
-
-        for i in far_first:
-            d, e = z_steps[i]
-            send(line_u.at[it, z_of(d), sib_rows if e else own_rows], from_r3.at[it, i], 3, u3.at[it], z_line[i])
-        answer_rr = rr / quad_fin()
-        answer[...] = answer[...] + answer_rr * p
+            for i in range(15):
+                if z_steps[i][0] == d:
+                    rows_ = sib_rows if z_steps[i][1] else own_rows
+                    send(line_u.at[it, zz, rows_], from_r3.at[it, i], 3, u3.at[it], z_line[i])
+        alpha = rr / quad_fin()
+        answer[...] = answer[...] + alpha * p
         wait_bytes(from_r3.at[it], u3.at[it])
         v = line_u[it, z, own_rows, :]
         for i in range(7):
@@ -334,7 +335,7 @@
         for i in range(8, 15):
             v = v + from_r3[it, i]
         whole[sib_rows, :] = v
-        res[...] = r - answer_rr * (dp + whole[...] * (1.0 / M))
+        res[...] = r - alpha * (dp + whole[...] * (1.0 / M))
 
         wait_bytes(span.at[0:240], sends.at[0])
         wait_bytes(half.at[0, 0:960], sends.at[1])
@@ -365,16 +366,16 @@
             pltpu.VMEM((8, M, 512), BF16),
             pltpu.VMEM((2, 2, NY, NZ, 2, 32, LANE), BF16),
             pltpu.VMEM((2, 2, NY, NZ, 2, 32, LANE), BF16),
-            pltpu.VMEM((2, 3, 4, NZ, 32, LANE), BF16),
+            pltpu.VMEM((2, 12, NZ, 32, LANE), BF16),
             pltpu.VMEM((2, 3, NZ, 32, LANE), BF16),
-            pltpu.VMEM((2, 3, NZ, 32, LANE), BF16),
+            pltpu.VMEM((2, NZ, 3, 32, LANE), BF16),
             pltpu.VMEM((2, NZ, 32, LANE), F32),
             pltpu.VMEM((2, 15, 16, LANE), F32),
             pltpu.VMEM((2, 32, LANE), BF16),
             pltpu.VMEM((32, LANE), F32),
             pltpu.VMEM((256, M), BF16),
             pltpu.VMEM((256, M), BF16),
-            pltpu.VMEM((2, LANE, M), F32),
+            pltpu.VMEM((LANE, M), F32),
             pltpu.VMEM((2, 8, 8, LANE), F32),
             pltpu.VMEM((2, 8, 8, LANE), F32),
             pltpu.VMEM((8, 8, LANE), F32),
@@ -387,7 +388,7 @@
             pltpu.VMEM((2, 42, 1, LANE), F32),
             pltpu.VMEM((240, LANE), BF16),
             pltpu.SemaphoreType.DMA, pltpu.SemaphoreType.DMA, pltpu.SemaphoreType.DMA,
-            dma(2, 15), dma(2, 6), dma(2, 3, 3), dma(2, 3, 4), dma(2, 3), dma(2), dma(2), dma(2, 6), dma(6),
+            dma(2, NZ), dma(2, 6), dma(2, 3), dma(2, 2), dma(2, NZ), dma(2), dma(2), dma(2, 6), dma(6),
         ],
         compiler_params=pltpu.CompilerParams(
             collective_id=0, has_side_effects=True, vmem_limit_bytes=56 * 2**20

time: 94.2 us -> 89.9 us (0.954)
  Pallas kernels: 91.9 us -> 87.6 us
    pallas_call x1, Pallas kernels: 91.9 us -> 87.6 us  [per_device(): pl.pallas_call(kernel, out_shape=jax.ShapeDtypeStruct((8, M), F32), in_sp...]
where the time goes in v3:
time: 89.9 us; the launch traced here: 89.7 us
  Pallas kernels  87.6 us (97%)
  local copies, waits for them, and re-layouts  1.45 us (2%)
    pallas_call x1, Pallas kernels, per_device(): pl.pallas_call(kernel, out_shape=jax.ShapeDtypeStruct((8, M), F32), in_sp...  87.6 us

profile of v3, /device:TPU:1, one launch (start us, length us, event | category | flops | bytes accessed | tf_op | source)
XLA Modules:
  0.0 89.7 jit_solution(6279733492344883619)
XLA Ops:
  0.6 87.6 %shard_map.68 = f32[8,1024]{1,0:T(8,128)} custom-call(bf16[4,1024,1024]{2,1,0:T(8,128)(2,1)} %ens.1, f32[4,1024]{1,0:T(4,128)} %rhs.1, f32[4,1024]{1,0:T(4,128)} %obs.1, s32[8,1024]{1,0:T(8,128)} %bitcast.2, f32[8,1024]{1,0:T(8,128)} %bitcast.3), custom_call_target="tpu_custom_call" | custom-call | tf_op jit(solution)/shard_map/pallas_call | solution.py:360
  88.2 1.5 %fusion = (f32[4,1024]{1,0:T(4,128)}, f32[4,1024]{1,0:T(4,128)}) fusion(f32[8,1024]{1,0:T(8,128)} %shard_map.68), kind=kLoop, calls=%fused_computation | loop fusion | bytes 65536 | tf_op jit(solution)/shard_map/slice | solution.py:397

commit v4 on v3

--- a/solution.py
+++ b/solution.py
@@ -162,11 +162,20 @@
             landed(chunk if d else chunk.at[sib_rows], r1s.at[it, d])
             for n in (2, 1, 3):
                 send(chunk, chunk, 1, r2s.at[it, n - 1], fwd(n))
+            if d in (0, 1, 7):
+                for n in (2, 1, 3):
+                    send(chunk, chunk, 1, r2s.at[it, 2 + n], cross(n))
+                for a, b in near:
+                    send(chunk, chunk, 1, r3s.at[it, jnp.where(first, b, a) - 1], diagonal(a, b))
         rr_fin = exchange(1, 15, rr_fin(), fwd_line)
-        for d in (2, 1, 3):
-            send(own_line, own_line, 1, r2s.at[it, 2 + d], cross(d))
-        for a, b in near:
-            send(own_line, own_line, 1, r3s.at[it, jnp.where(first, b, a) - 1], diagonal(a, b))
+        for d in (2, 6, 3, 5, 4):
+            chunk = own_line.at[z_of(NZ - d)]
+            for n in (2, 1, 3):
+                send(chunk, chunk, 1, r2s.at[it, 2 + n], cross(n))
+        for d in (2, 6, 3, 5, 4):
+            chunk = own_line.at[z_of(NZ - d)]
+            for a, b in near:
+                send(chunk, chunk, 1, r3s.at[it, jnp.where(first, b, a) - 1], diagonal(a, b))
 
         rr_fin = exchange(2, 18, rr_fin(), cross_line)
         for a in (1, 3, 2):

time: 89.9 us -> 87.8 us (0.977)
  Pallas kernels: 87.6 us -> 85.5 us
    pallas_call x1, Pallas kernels: 87.6 us -> 85.5 us  [per_device(): pl.pallas_call(kernel, out_shape=jax.ShapeDtypeStruct((8, M), F32), in_sp...]
where the time goes in v4:
time: 87.8 us; the launch traced here: 87.6 us
  Pallas kernels  85.5 us (97%)
  local copies, waits for them, and re-layouts  1.45 us (2%)
    pallas_call x1, Pallas kernels, per_device(): pl.pallas_call(kernel, out_shape=jax.ShapeDtypeStruct((8, M), F32), in_sp...  85.5 us

profile of v4, /device:TPU:1, one launch (start us, length us, event | category | flops | bytes accessed | tf_op | source)
XLA Modules:
  0.0 87.6 jit_solution(11235959512847780774)
XLA Ops:
  0.6 85.5 %shard_map.68 = f32[8,1024]{1,0:T(8,128)} custom-call(bf16[4,1024,1024]{2,1,0:T(8,128)(2,1)} %ens.1, f32[4,1024]{1,0:T(4,128)} %rhs.1, f32[4,1024]{1,0:T(4,128)} %obs.1, s32[8,1024]{1,0:T(8,128)} %bitcast.2, f32[8,1024]{1,0:T(8,128)} %bitcast.3), custom_call_target="tpu_custom_call" | custom-call | tf_op jit(solution)/shard_map/pallas_call | solution.py:369
  86.2 1.5 %fusion = (f32[4,1024]{1,0:T(4,128)}, f32[4,1024]{1,0:T(4,128)}) fusion(f32[8,1024]{1,0:T(8,128)} %shard_map.68), kind=kLoop, calls=%fused_computation | loop fusion | bytes 65536 | tf_op jit(solution)/shard_map/slice | solution.py:406

commit v5 on v4

--- a/solution.py
+++ b/solution.py
@@ -177,13 +177,13 @@
             for a, b in near:
                 send(chunk, chunk, 1, r3s.at[it, jnp.where(first, b, a) - 1], diagonal(a, b))
 
-        rr_fin = exchange(2, 18, rr_fin(), cross_line)
         for a in (1, 3, 2):
             landed(own_line, r2s.at[it, a - 1])
         for i, t in ((2, 1), (2, 3), (1, 2), (3, 2), (2, 2)):
             a, b = jnp.where(first, i, t), jnp.where(first, t, i)
             came = line(gath, it, jnp.where(first, x_of(NX - a), x), jnp.where(first, y, y_of(NY - a)))
             send(came, came, 1, r3s.at[it, t - 1], cross(b))
+        rr_fin = exchange(2, 18, rr_fin(), cross_line)
         for b in range(3):
             landed(own_line, r2s.at[it, 3 + b])
 

time: 87.8 us -> 87 us (level)
  no operation moved by 1% of the time
where the time goes in v5:
time: 87 us; the launch traced here: 86.8 us
  Pallas kernels  84.7 us (97%)
  local copies, waits for them, and re-layouts  1.45 us (2%)
    pallas_call x1, Pallas kernels, per_device(): pl.pallas_call(kernel, out_shape=jax.ShapeDtypeStruct((8, M), F32), in_sp...  84.7 us

profile of v5, /device:TPU:1, one launch (start us, length us, event | category | flops | bytes accessed | tf_op | source)
XLA Modules:
  0.0 86.8 jit_solution(11184118652764296466)
XLA Ops:
  0.6 84.7 %shard_map.68 = f32[8,1024]{1,0:T(8,128)} custom-call(bf16[4,1024,1024]{2,1,0:T(8,128)(2,1)} %ens.1, f32[4,1024]{1,0:T(4,128)} %rhs.1, f32[4,1024]{1,0:T(4,128)} %obs.1, s32[8,1024]{1,0:T(8,128)} %bitcast.2, f32[8,1024]{1,0:T(8,128)} %bitcast.3), custom_call_target="tpu_custom_call" | custom-call | tf_op jit(solution)/shard_map/pallas_call | solution.py:369
  85.4 1.5 %fusion = (f32[4,1024]{1,0:T(4,128)}, f32[4,1024]{1,0:T(4,128)}) fusion(f32[8,1024]{1,0:T(8,128)} %shard_map.68), kind=kLoop, calls=%fused_computation | loop fusion | bytes 65536 | tf_op jit(solution)/shard_map/slice | solution.py:406
